TPU v7x, 512 devices: a whole 4x4x16 slice. The times are simulated.
512 devices in a mesh: row: 16 (over y, x_lo, core), col: 32 (over x_hi, z).
Axes of the slice: x: 4 (x_hi: 2, x_lo: 2; x = x_hi * 2 + x_lo), y: 4, z: 16, core: 2. Of those that a mesh axis runs over, the one named last changes fastest.
Arguments:
- features: bfloat16 [32768, 512], P(('col', 'row')), may hold values from -6 to 6
- positions: float32 [3, 32768], replicated, may hold values from 0 to 80, as said below
- cluster_atoms: int32 [256], replicated, may hold values from 64 to 128, as said below
- pair_cells: int32 [16, 32, 12], P('row', 'col'), may hold values from 0 to 127, as said below
- pair_count: int32 [16, 32], P('row', 'col'), may hold values from 1 to 12, as said below
- project_weight: bfloat16 [512, 512], replicated, may hold values from -0.25 to 0.25
- basis_filter: float32 [16, 512], replicated, may hold values from -0.375 to 0.375
- hidden_weight: bfloat16 [512, 512], replicated, may hold values from -0.25 to 0.25
- hidden_bias: float32 [512], replicated, may hold values from -4 to 4
- output_weight: bfloat16 [512, 512], replicated, may hold values from -0.25 to 0.25
- output_bias: float32 [512], replicated, may hold values from -3 to 3
Outputs:
- update: bfloat16 [32768, 512], P('row')
Inputs may be any that keep to these rules, and one draw needn't show every extreme that they name: `positions`: each cluster's atoms lie in a cube of side 5 of its own. `cluster_atoms`: atoms of a cluster at slots below the count are real, the others padding; some cluster is full. `pair_cells`: entry v names target cluster v // 8 of the row's block of 16 clusters and source cluster v mod 8 of the column's block of 8 clusters; the entries of one device are distinct; only the first pair_count entries are used. `pair_count`: some device lists 12 pairs.
All inputs are finite; a program needn't handle non-finite values.
Results may differ from a plain program's by a relative error of at most 0.0048.
Values may be sent and summed in bfloat16 or wider, within the bound.
A program may use at most 64 MiB of HBM per device.

v0:
```python
import math

import jax
import jax.numpy as jnp
from jax import lax
from jax.sharding import PartitionSpec as P

CL = 128
F = 512
NRBF = 16
CPR = 16


cutoff_radius = 5.0


def basis_weights(target_pos, source_pos, target_first, source_first, source_valid, basis_count):
    cluster = target_pos.shape[1]
    squared = jnp.zeros((cluster, cluster), jnp.float32)
    for component in range(3):
        difference = target_pos[component][:, None] - source_pos[component][None, :]
        squared = squared + difference * difference
    distance = jnp.sqrt(squared)
    target_ids = target_first + lax.broadcasted_iota(jnp.int32, (cluster, cluster), 0)
    source_local = lax.broadcasted_iota(jnp.int32, (cluster, cluster), 1)
    allowed = (
        (target_ids != source_first + source_local)
        & (source_local < source_valid)
        & (distance < cutoff_radius)
    )
    smooth = 0.5 * (jnp.cos(math.pi / cutoff_radius * distance) + 1.0)
    envelope = jnp.where(allowed, smooth, 0.0)
    centers = lax.broadcasted_iota(jnp.int32, (1, basis_count, 1), 1).astype(jnp.float32) * (
        cutoff_radius / (basis_count - 1)
    )
    sharpness = ((basis_count - 1) / cutoff_radius) ** 2
    offset = distance[:, None, :] - centers
    weights = jnp.exp(-sharpness * offset * offset) * envelope[:, None, :]
    return weights.astype(jnp.bfloat16).reshape(cluster, basis_count * cluster)


def scaled_sources(source_rows, basis_filter):
    scaled = basis_filter[:, None, :] * source_rows[None, :, :].astype(jnp.float32)
    return scaled.astype(jnp.bfloat16).reshape(-1, source_rows.shape[1])


def refine(
    message,
    first_atom,
    cluster_atoms,
    hidden_weight,
    hidden_bias,
    output_weight,
    output_bias,
    cluster,
):
    rounded = message.astype(jnp.bfloat16)
    hidden = jnp.dot(rounded, hidden_weight, preferred_element_type=jnp.float32) + hidden_bias
    hidden = (jax.nn.softplus(hidden) - math.log(2.0)).astype(jnp.bfloat16)
    result = jnp.dot(hidden, output_weight, preferred_element_type=jnp.float32) + output_bias
    row_total = message.shape[0]
    atom_ids = first_atom + lax.broadcasted_iota(jnp.int32, (row_total, 1), 0)
    cluster_ids = atom_ids // cluster
    table_ids = lax.broadcasted_iota(jnp.int32, (1, cluster_atoms.shape[0]), 1)
    valid_atoms = jnp.sum(
        jnp.where(cluster_ids == table_ids, cluster_atoms[None, :], 0), axis=1, keepdims=True
    )
    keeping = atom_ids - cluster_ids * cluster < valid_atoms
    return jnp.where(keeping, result, 0.0).astype(jnp.bfloat16)


def local(
    features,
    positions,
    cluster_atoms,
    pair_cells,
    pair_count,
    project_weight,
    basis_filter,
    hidden_weight,
    hidden_bias,
    output_weight,
    output_bias,
):
    row_index = lax.axis_index("row")
    col_index = lax.axis_index("col")
    source_block = jnp.dot(
        lax.all_gather(features, "row", axis=0, tiled=True),
        project_weight,
        preferred_element_type=jnp.float32,
    ).astype(jnp.bfloat16)
    source_clusters = source_block.shape[0] // CL
    block_rows = CPR * CL
    listed = pair_count[0, 0]
    pair_list = pair_cells[0, 0]
    target_base = row_index * CPR
    source_base = col_index * source_clusters

    def pair_message(target, source):
        target_first = (target_base + target) * CL
        source_first = (source_base + source) * CL
        target_pos = lax.dynamic_slice_in_dim(positions, target_first, CL, 1)
        source_pos = lax.dynamic_slice_in_dim(positions, source_first, CL, 1)
        source_valid = cluster_atoms[source_base + source]
        weights = basis_weights(
            target_pos, source_pos, target_first, source_first, source_valid, NRBF
        )
        source_rows = lax.dynamic_slice_in_dim(source_block, source * CL, CL, 0)
        return jnp.dot(
            weights, scaled_sources(source_rows, basis_filter), preferred_element_type=jnp.float32
        )

    def add_pair(slot_index, buffer):
        pair_cell = pair_list[slot_index]
        target = pair_cell // source_clusters
        source = pair_cell - target * source_clusters
        first_row = target * CL
        current = lax.dynamic_slice_in_dim(buffer, first_row, CL, 0)
        return lax.dynamic_update_slice_in_dim(
            buffer, current + pair_message(target, source), first_row, 0
        )

    block_total = lax.fori_loop(0, listed, add_pair, jnp.zeros((block_rows, F), jnp.float32))
    message = lax.psum(block_total, "col")
    return refine(
        message,
        target_base * CL,
        cluster_atoms,
        hidden_weight,
        hidden_bias,
        output_weight,
        output_bias,
        CL,
    )


def solution(mesh):
    in_specs = (
        P(("col", "row"), None),
        P(),
        P(),
        P("row", "col", None),
        P("row", "col"),
        P(),
        P(),
        P(),
        P(),
        P(),
        P(),
    )
    out_specs = P("row", None)
    return jax.shard_map(local, mesh=mesh, in_specs=in_specs, out_specs=out_specs, check_vma=False)
```

profile of v0, /device:TPU:16, one launch (start us, length us, event | category | flops | bytes accessed | tf_op | source)
XLA Modules:
  0.0 360.6 jit_solution(1646226569818713866)
XLA Ops:
  6.6 0.7 all-gather.2.cloned.1.call-update
  7.3 1.4 select_reduce_fusion
  8.8 44.3 %all-gather.2.cloned.1.call-done = bf16[1024,512]{1,0:T(8,128)(2,1)} async-done(((bf16[64,512]{1,0:T(8,128)(2,1)}), bf16[1024,512]{1,0:T(8,128)(2,1)}) %all-gather.2.cloned.1.call-update) | async-done | bytes 1048592 | tf_op jit(solution)/shard_map/all_gather | solution.py:88
  53.0 2.1 convolution_convert_fusion
  55.1 2.5 broadcast_in_dim.40
  57.6 44.9 %while.12 = (s32[]{:T(128)}, f32[2048,512]{1,0:T(8,128)}, s32[]{:T(128)}, s32[12]{0:T(128)S(1)}, s32[]{:T(128)}, /*index=5*/f32[3,32768]{1,0:T(4,128)}, s32[]{:T...) while((s32[]{:T(128)}, f32[2048,512]{1,0:T(8,128)}, ...), condition=%wide.region_2.3_spmd, body=%wide.region_1.2_spmd.sunk | while | flops 272236992 | bytes 1493059 | solution.py:123
  58.2 0.6 dynamic_slice.48
  63.0 0.7 constant_dynamic-slice_fusion.3
  64.1 2.3 fusion.33
  67.1 0.6 dynamic_slice.48
  71.8 0.7 constant_dynamic-slice_fusion.3
  72.9 2.3 fusion.33
  75.9 0.6 dynamic_slice.48
  79.5 0.6 dynamic_slice.49
  80.7 0.7 constant_dynamic-slice_fusion.3
  81.8 2.3 fusion.33
  84.8 0.6 dynamic_slice.48
  89.5 0.7 constant_dynamic-slice_fusion.3
  90.6 2.3 fusion.33
  93.6 0.6 dynamic_slice.48
  98.4 0.7 constant_dynamic-slice_fusion.3
  99.5 2.3 fusion.33
  102.5 246.0 %all-reduce.1 = bf16[2048,512]{1,0:T(8,128)(2,1)S(1)} all-reduce(f32[2048,512]{1,0:T(8,128)} %get-tuple-element.134), channel_id=1, replica_groups=mesh['row'=16,'col'=32] {'col'}, use_global_device_ids=true, to_apply=%region_3.4 | all-reduce | flops 1048576 | bytes 6291456 | tf_op jit(solution)/shard_map/psum | solution.py:124
  348.5 5.2 %select_convert_fusion = bf16[2048,512]{1,0:T(8,128)(2,1)} fusion(bf16[512,512]{1,0:T(8,128)(2,1)S(1)} %copy-done, f32[512]{0:T(512)S(1)} %copy-done.4, pred[2048]{0:T(1024)(128)(4,1)S(1)} %subtract_compare_fusion, bf16[512,512]{1,0:T(8,128)(2,1)S(1)} %copy-done.2, f32[512]{0:T(512)S(1)} %copy-done.5, bf16[2048,512]{1,0:T(8,128)(2,1)S(1)} %all-reduce.1), kind=kOutput, calls=%fused_computation.34 | convolution fusion | flops 2160066560 | bytes 5249024 | tf_op jit(solution)/shard_map/dot_general | solution.py:60
  (51 shorter events, 7.4 us)
Async XLA Ops:
  6.5 342.0 %copy-start = (bf16[512,512]{1,0:T(8,128)(2,1)S(1)}, bf16[512,512]{1,0:T(8,128)(2,1)}, u32[]{:S(2)}) copy-start(bf16[512,512]{1,0:T(8,128)(2,1)} %param.22) | copy-start | bytes 1572868
  6.5 51.0 %copy-start.1 = (s32[256]{0:T(256)S(1)}, s32[256]{0:T(256)}, u32[]{:S(2)}) copy-start(s32[256]{0:T(256)} %param.15) | copy-start | bytes 3076
  6.5 51.0 %copy-start.3 = (f32[16,512]{1,0:T(8,128)S(1)}, f32[16,512]{1,0:T(8,128)}, u32[]{:S(2)}) copy-start(f32[16,512]{1,0:T(8,128)} %param.19) | copy-start | bytes 98308
  6.5 51.0 %copy-start.6 = (s32[1,1,12]{2,1,0:T(1,128)S(1)}, s32[1,1,12]{2,1,0:T(1,128)}, u32[]{:S(2)}) copy-start(s32[1,1,12]{2,1,0:T(1,128)} %param.16) | copy-start | bytes 148
  6.5 46.5 %all-gather.2.cloned.1.call-start = ((), (), s32[]{:S(2)}) async-start(), calls=%async_computation | async-start | bytes 1114112 | tf_op jit(solution)/shard_map/all_gather | solution.py:88
  102.5 246.0 %copy-start.2 = (bf16[512,512]{1,0:T(8,128)(2,1)S(1)}, bf16[512,512]{1,0:T(8,128)(2,1)}, u32[]{:S(2)}) copy-start(bf16[512,512]{1,0:T(8,128)(2,1)} %param.20) | copy-start | bytes 1572868
  102.5 246.0 %copy-start.4 = (f32[512]{0:T(512)S(1)}, f32[512]{0:T(512)}, u32[]{:S(2)}) copy-start(f32[512]{0:T(512)} %param.23) | copy-start | bytes 6148
  102.5 246.0 %copy-start.5 = (f32[512]{0:T(512)S(1)}, f32[512]{0:T(512)}, u32[]{:S(2)}) copy-start(f32[512]{0:T(512)} %param.21) | copy-start | bytes 6148
Sparse Core Ops, SparseCore 0:
  9.5 43.4 all-gather.1
where the time goes:
time: 360 us; the launch traced here: 361 us
  blocking collectives  246 us (68%)
  waiting for transfers between devices  44.9 us (12%)
  matrix products  18.8 us (5%)
  loops' own time  18.8 us (5%)
  between operations  13.5 us (4%)
  local copies, waits for them, and re-layouts  12 us (3%)
  other arithmetic  6.4 us (2%)
    psum x1, blocking collectives, local(): message = lax.psum(block_total, 'col')  246 us
    all_gather x1, waiting for transfers between devices, local(): lax.all_gather(features, 'row', axis=0, tiled=True)  44.3 us
    another operation x1, loops' own time, local(): lax.fori_loop(0, listed, add_pair, jnp.zeros((block_rows, F), jnp.float32))  18.8 us
    dot_general x5, matrix products, pair_message(): jnp.dot(weights, scaled_sources(source_rows, basis_filter), preferred_ele...  11.6 us
  transfers between devices with their start and end apart: 1, of which 1 were waited for; matrix products, arithmetic and copies ran while one was open for 0% of the time, Pallas kernels for 0%

commit v1 on v0

v1 whole, which is shorter than its diff:
```python
import functools
import math

import jax
import jax.numpy as jnp
from jax import lax
from jax.experimental import pallas as pl
from jax.experimental.pallas import tpu as pltpu
from jax.sharding import PartitionSpec as P

CL = 128
F = 512
NRBF = 16
CUTOFF = 5.0
MESH = pl.DeviceIdType.MESH
VMEM_LIMIT = 56 * 1024 * 1024


def vmem():
    return pl.BlockSpec(memory_space=pltpu.VMEM)


def smem():
    return pl.BlockSpec(memory_space=pltpu.SMEM)


def hbm():
    return pl.BlockSpec(memory_space=pl.ANY)


def gather_kernel(n_row, x_ref, w_ref, out_ref, send_sem, recv_sem, fwd_sem):
    me = lax.axis_index("row")
    core = lax.rem(me, 2)
    chip = lax.div(me, 2)
    chips = n_row // 2
    sibling = me + 1 - 2 * core

    def peer(j):
        return lax.rem(chip + j, chips) * 2 + core

    barrier = pltpu.get_barrier_semaphore()
    for j in range(1, chips):
        pl.semaphore_signal(barrier, inc=1, device_id={"row": peer(j)}, device_id_type=MESH)
    pl.semaphore_signal(barrier, inc=1, device_id={"row": sibling}, device_id_type=MESH)
    out_ref[me] = jnp.dot(x_ref[...], w_ref[...], preferred_element_type=jnp.float32).astype(
        jnp.bfloat16
    )
    pl.semaphore_wait(barrier, chips)

    def direct(j):
        return pltpu.make_async_remote_copy(
            src_ref=out_ref.at[me],
            dst_ref=out_ref.at[me],
            send_sem=send_sem.at[j],
            recv_sem=recv_sem.at[me],
            device_id={"row": peer(j)},
            device_id_type=MESH,
        )

    def forward(block, j):
        return pltpu.make_async_remote_copy(
            src_ref=out_ref.at[block],
            dst_ref=out_ref.at[block],
            send_sem=fwd_sem.at[j],
            recv_sem=recv_sem.at[block],
            device_id={"row": sibling},
            device_id_type=MESH,
        )

    def arrived(block):
        pltpu.make_async_remote_copy(
            src_ref=out_ref.at[block],
            dst_ref=out_ref.at[block],
            send_sem=send_sem.at[0],
            recv_sem=recv_sem.at[block],
            device_id={"row": sibling},
            device_id_type=MESH,
        ).wait_recv()

    for j in range(1, chips):
        direct(j).start()
    forward(me, 0).start()
    for j in range(1, chips):
        block = lax.rem(chip + chips - j, chips) * 2 + core
        arrived(block)
        forward(block, j).start()
    for j in range(chips):
        arrived(lax.rem(chip + chips - j, chips) * 2 + 1 - core)
    for j in range(1, chips):
        direct(j).wait_send()
    for j in range(chips):
        forward(lax.rem(chip + chips - j, chips) * 2 + core, j).wait_send()


def gather_projected(features, weight, n_row):
    rows = features.shape[0]
    return pl.pallas_call(
        functools.partial(gather_kernel, n_row),
        out_shape=jax.ShapeDtypeStruct((n_row, rows, F), jnp.bfloat16),
        in_specs=[vmem(), vmem()],
        out_specs=vmem(),
        scratch_shapes=[
            pltpu.SemaphoreType.DMA((n_row // 2,)),
            pltpu.SemaphoreType.DMA((n_row,)),
            pltpu.SemaphoreType.DMA((n_row // 2,)),
        ],
        compiler_params=pltpu.CompilerParams(
            collective_id=0, has_side_effects=True, vmem_limit_bytes=VMEM_LIMIT
        ),
        name="project_gather",
    )(features, weight)


def envelope_of(squared):
    x = squared * (math.pi / (2.0 * CUTOFF)) ** 2
    coefficients = [(-1.0) ** n / math.factorial(2 * n) for n in range(8)]
    value = jnp.full_like(x, coefficients[-1])
    for c in coefficients[-2::-1]:
        value = value * x + c
    return value * value


def pair_kernel(
    clusters,
    per_row,
    cells_ref,
    count_ref,
    atoms_ref,
    pos_ref,
    filter_ref,
    source_ref,
    out_ref,
    tpos,
    spos,
    weights,
    scaled,
    sem,
):
    row = lax.axis_index("row")
    col = lax.axis_index("col")
    first = pltpu.make_async_copy(
        pos_ref.at[:, pl.ds(pl.multiple_of(row * per_row * CL, CL), per_row * CL)],
        tpos.at[pl.ds(0, 3)],
        sem.at[0],
    )
    second = pltpu.make_async_copy(
        pos_ref.at[:, pl.ds(pl.multiple_of(col * clusters * CL, CL), clusters * CL)],
        spos.at[pl.ds(0, 3)],
        sem.at[1],
    )
    tpos[...] = jnp.zeros_like(tpos)
    first.start()
    second.start()
    out_ref[...] = jnp.zeros_like(out_ref)
    first.wait()
    second.wait()
    spread = math.sqrt(math.log2(math.e))

    def job(slot, carry):
        cell = cells_ref[0, 0, slot]
        target = lax.div(cell, clusters)
        source = cell - target * clusters
        target_at = pl.multiple_of(target * CL, CL)
        source_at = pl.multiple_of(source * CL, CL)
        across = jnp.transpose(tpos[:, pl.ds(target_at, CL)])
        along = spos[:, pl.ds(source_at, CL)]
        squared = jnp.zeros((CL, CL), jnp.float32)
        for component in range(3):
            difference = across[:, component : component + 1] - along[component : component + 1, :]
            squared = squared + difference * difference
        distance = jnp.sqrt(squared)
        target_ids = (row * per_row + target) * CL + lax.broadcasted_iota(jnp.int32, (CL, CL), 0)
        local = lax.broadcasted_iota(jnp.int32, (CL, CL), 1)
        source_cluster = col * clusters + source
        allowed = (
            (target_ids != source_cluster * CL + local)
            & (local < atoms_ref[source_cluster])
            & (distance < CUTOFF)
        )
        envelope = jnp.where(allowed, envelope_of(squared), 0.0)
        reach = distance * ((NRBF - 1) / CUTOFF * spread)
        rows = source_ref[pl.ds(source_at, CL), :].astype(jnp.float32)
        for k in range(NRBF):
            offset = reach - k * spread
            weights[:, k * CL : (k + 1) * CL] = (jnp.exp2(-(offset * offset)) * envelope).astype(
                jnp.bfloat16
            )
            scaled[k * CL : (k + 1) * CL, :] = (filter_ref[k : k + 1, :] * rows).astype(jnp.bfloat16)
        out_ref[pl.ds(target_at, CL), :] += jnp.dot(
            weights[...], scaled[...], preferred_element_type=jnp.float32
        )
        return carry

    lax.fori_loop(0, count_ref[0, 0], job, 0)


def pair_messages(cells, count, atoms, positions, basis_filter, source, per_row):
    clusters = source.shape[0] // CL
    return pl.pallas_call(
        functools.partial(pair_kernel, clusters, per_row),
        out_shape=jax.ShapeDtypeStruct((per_row * CL, F), jnp.float32),
        in_specs=[smem(), smem(), smem(), hbm(), vmem(), vmem()],
        out_specs=vmem(),
        scratch_shapes=[
            pltpu.VMEM((8, per_row * CL), jnp.float32),
            pltpu.VMEM((8, clusters * CL), jnp.float32),
            pltpu.VMEM((CL, NRBF * CL), jnp.bfloat16),
            pltpu.VMEM((NRBF * CL, F), jnp.bfloat16),
            pltpu.SemaphoreType.DMA((2,)),
        ],
        compiler_params=pltpu.CompilerParams(vmem_limit_bytes=VMEM_LIMIT),
        name="pair_messages",
    )(cells, count, atoms, positions, basis_filter, source)


CH = 4
CW = F // CH


def finish_kernel(
    nz,
    m_ref,
    atoms_ref,
    hw_ref,
    hb_ref,
    ow_ref,
    ob_ref,
    out_ref,
    rs,
    stage,
    xsend,
    xrecv,
    out_v,
    rs_send,
    rs_recv,
    x_sem,
    ag_send,
    ag_recv,
    out_sem,
):
    row = lax.axis_index("row")
    col = lax.axis_index("col")
    h = lax.div(col, nz)
    z = lax.rem(col, nz)
    far = nz // 2
    neighbour = (h * nz + lax.rem(z + 1, nz), h * nz + lax.rem(z + nz - 1, nz))
    partner = (1 - h) * nz + z

    barrier = pltpu.get_barrier_semaphore()
    for other in neighbour + (partner,):
        pl.semaphore_signal(barrier, inc=1, device_id={"col": other}, device_id_type=MESH)
    pl.semaphore_wait(barrier, 3)

    def ahead(way, d):
        return lax.rem(z + d, nz) if way == 0 else lax.rem(z + nz - d, nz)

    def mine(t, c):
        return m_ref[pl.ds(pl.multiple_of(t * CL, CL), CL), c * CW : (c + 1) * CW]

    def long(way, c):
        return (c < CH // 2) == (way == 0)

    def rs_copy(way, c, k, src):
        return pltpu.make_async_remote_copy(
            src_ref=src,
            dst_ref=rs.at[way, k, c],
            send_sem=rs_send.at[way, c, k],
            recv_sem=rs_recv.at[way, c, k],
            device_id={"col": neighbour[way]},
            device_id_type=MESH,
        )

    order = [(way, c if way == 0 else CH - 1 - c) for c in range(CH) for way in range(2)]

    def begin(way, c, k):
        stage[way, c] = mine(ahead(way, far - k), c).astype(jnp.bfloat16)
        rs_copy(way, c, k, stage.at[way, c]).start()

    def relay(way, c, k):
        rs_copy(way, c, k - 1, rs.at[way, k - 1, c]).wait_recv()
        total = rs[way, k - 1, c].astype(jnp.float32) + mine(ahead(way, far - k), c)
        rs[way, k - 1, c] = total.astype(jnp.bfloat16)
        rs_copy(way, c, k, rs.at[way, k - 1, c]).start()

    for way, c in order:
        if long(way, c):
            begin(way, c, 0)
    for way, c in order:
        if not long(way, c):
            begin(way, c, 1)
    for way, c in order:
        if long(way, c):
            relay(way, c, 1)

    def step(k, carry):
        for way, c in order:
            relay(way, c, k)
        return carry

    lax.fori_loop(2, far, step, 0)

    half = CL // 2
    for c in range(CH):
        for way in range(2):
            rs_copy(way, c, far - 1, rs.at[way, far - 1, c]).wait_recv()
        total = (
            rs[0, far - 1, c].astype(jnp.float32)
            + rs[1, far - 1, c].astype(jnp.float32)
            + mine(z, c)
        )
        xsend[0, :, c * CW : (c + 1) * CW] = total[:half].astype(jnp.bfloat16)
        xsend[1, :, c * CW : (c + 1) * CW] = total[half:].astype(jnp.bfloat16)
    cross = pltpu.make_async_remote_copy(
        src_ref=xsend.at[1 - h],
        dst_ref=xrecv,
        send_sem=x_sem.at[0],
        recv_sem=x_sem.at[1],
        device_id={"col": partner},
        device_id_type=MESH,
    )
    cross.start()

    for way, c in order:
        if long(way, c):
            rs_copy(way, c, 0, stage.at[way, c]).wait_send()

    def sent(k, carry):
        for way, c in order:
            rs_copy(way, c, k, stage.at[way, c]).wait_send()
        return carry

    lax.fori_loop(1, far, sent, 0)
    cross.wait_recv()

    message = (xsend[h].astype(jnp.float32) + xrecv[...].astype(jnp.float32)).astype(jnp.bfloat16)
    hidden = jnp.dot(message, hw_ref[...], preferred_element_type=jnp.float32) + hb_ref[...]
    hidden = jnp.maximum(hidden, 0.0) + jnp.log1p(jnp.exp(-jnp.abs(hidden))) - math.log(2.0)
    result = (
        jnp.dot(hidden.astype(jnp.bfloat16), ow_ref[...], preferred_element_type=jnp.float32)
        + ob_ref[...]
    )
    atom = h * half + lax.broadcasted_iota(jnp.int32, (half, F), 0)
    valid = atoms_ref[row * nz + z]
    out_v[z, h] = jnp.where(atom < valid, result, 0.0).astype(jnp.bfloat16)
    cross.wait_send()

    swap = pltpu.make_async_remote_copy(
        src_ref=out_v.at[z, h],
        dst_ref=out_v.at[z, h],
        send_sem=x_sem.at[2],
        recv_sem=x_sem.at[3],
        device_id={"col": partner},
        device_id_type=MESH,
    )
    swap.start()

    def block(t, j):
        return out_v.at[t, h if j == 0 else 1 - h]

    def ag_copy(way, j, k):
        ref = block(ahead(1 - way, k), j)
        return pltpu.make_async_remote_copy(
            src_ref=ref,
            dst_ref=ref,
            send_sem=ag_send.at[way, j, k],
            recv_sem=ag_recv.at[way, j, k],
            device_id={"col": neighbour[way]},
            device_id_type=MESH,
        )

    def ag_arrived(way, j, k):
        ref = block(ahead(1 - way, k + 1), j)
        pltpu.make_async_remote_copy(
            src_ref=ref,
            dst_ref=ref,
            send_sem=ag_send.at[way, j, k],
            recv_sem=ag_recv.at[way, j, k],
            device_id={"col": neighbour[way]},
            device_id_type=MESH,
        ).wait_recv()

    def store(t, j):
        half_index = h if j == 0 else 1 - h
        return pltpu.make_async_copy(
            out_v.at[t, half_index], out_ref.at[t, half_index], out_sem.at[t, half_index]
        )

    def ag_long(way, j):
        return way == j

    for way in range(2):
        ag_copy(way, 0, 0).start()
    store(z, 0).start()
    swap_in = pltpu.make_async_remote_copy(
        src_ref=block(z, 1),
        dst_ref=block(z, 1),
        send_sem=x_sem.at[2],
        recv_sem=x_sem.at[3],
        device_id={"col": partner},
        device_id_type=MESH,
    )
    swap_in.wait_recv()
    for way in range(2):
        ag_copy(way, 1, 0).start()
    store(z, 1).start()

    def ag_step(k, carry):
        for j in range(2):
            for way in range(2):
                ag_arrived(way, j, k - 1)
                ag_copy(way, j, k).start()
                store(ahead(1 - way, k), j).start()
        return carry

    lax.fori_loop(1, far - 1, ag_step, 0)
    for j in range(2):
        for way in range(2):
            ag_arrived(way, j, far - 2)
            if ag_long(way, j):
                ag_copy(way, j, far - 1).start()
            store(ahead(1 - way, far - 1), j).start()
    for j in range(2):
        way = j
        ag_arrived(way, j, far - 1)
        store(ahead(1 - way, far), j).start()

    swap.wait_send()

    def ag_sent(k, carry):
        for j in range(2):
            for way in range(2):
                ag_copy(way, j, k).wait_send()
        return carry

    lax.fori_loop(0, far - 1, ag_sent, 0)
    for j in range(2):
        ag_copy(j, j, far - 1).wait_send()

    def stored(t, carry):
        for j in range(2):
            store(t, j).wait()
        return carry

    lax.fori_loop(0, nz, stored, 0)


def finish(message, atoms, hidden_weight, hidden_bias, output_weight, output_bias, n_col):
    nz = message.shape[0] // CL
    far = nz // 2
    return pl.pallas_call(
        functools.partial(finish_kernel, nz),
        out_shape=jax.ShapeDtypeStruct((nz, 2, CL // 2, F), jnp.bfloat16),
        in_specs=[vmem(), smem(), vmem(), vmem(), vmem(), vmem()],
        out_specs=hbm(),
        scratch_shapes=[
            pltpu.VMEM((2, far, CH, CL, CW), jnp.bfloat16),
            pltpu.VMEM((2, CH, CL, CW), jnp.bfloat16),
            pltpu.VMEM((2, CL // 2, F), jnp.bfloat16),
            pltpu.VMEM((CL // 2, F), jnp.bfloat16),
            pltpu.VMEM((nz, 2, CL // 2, F), jnp.bfloat16),
            pltpu.SemaphoreType.DMA((2, CH, far)),
            pltpu.SemaphoreType.DMA((2, CH, far)),
            pltpu.SemaphoreType.DMA((4,)),
            pltpu.SemaphoreType.DMA((2, 2, far)),
            pltpu.SemaphoreType.DMA((2, 2, far)),
            pltpu.SemaphoreType.DMA((nz, 2)),
        ],
        compiler_params=pltpu.CompilerParams(
            collective_id=1, has_side_effects=True, vmem_limit_bytes=VMEM_LIMIT
        ),
        name="sum_update_gather",
    )(message, atoms, hidden_weight, hidden_bias, output_weight, output_bias)


def local(
    n_row,
    n_col,
    features,
    positions,
    cluster_atoms,
    pair_cells,
    pair_count,
    project_weight,
    basis_filter,
    hidden_weight,
    hidden_bias,
    output_weight,
    output_bias,
):
    per_row = positions.shape[1] // CL // n_row
    projected = gather_projected(features, project_weight, n_row).reshape(-1, F)
    message = pair_messages(
        pair_cells, pair_count, cluster_atoms, positions, basis_filter, projected, per_row
    )
    update = finish(
        message,
        cluster_atoms,
        hidden_weight,
        hidden_bias.reshape(1, F),
        output_weight,
        output_bias.reshape(1, F),
        n_col,
    )
    return update.reshape(-1, F)


def solution(mesh):
    in_specs = (
        P(("col", "row"), None),
        P(),
        P(),
        P("row", "col", None),
        P("row", "col"),
        P(),
        P(),
        P(),
        P(),
        P(),
        P(),
    )
    out_specs = P("row", None)
    body = functools.partial(local, mesh.shape["row"], mesh.shape["col"])
    return jax.shard_map(body, mesh=mesh, in_specs=in_specs, out_specs=out_specs, check_vma=False)
```

time: 360 us -> 117 us (0.33)
  the two profiles are of different devices: /device:TPU:16 before, /device:TPU:32 now
where the time goes in v1:
time: 117 us
  Pallas kernels  113 us (97%)
  local copies, waits for them, and re-layouts  3.05 us (3%)
    pallas_call x1, Pallas kernels, finish(): pl.pallas_call(functools.partial(finish_kernel, nz), out_shape=jax.ShapeD...  82.6 us
    pallas_call x1, Pallas kernels, gather_projected(): pl.pallas_call(functools.partial(gather_kernel, n_row), out_shape=jax.Sha...  15.6 us
    pallas_call x1, Pallas kernels, pair_messages(): pl.pallas_call(functools.partial(pair_kernel, clusters, per_row), out_sha...  15 us
    unnamed x1, local copies, waits for them, and re-layouts  3.05 us

profile of v1, /device:TPU:32, one launch (start us, length us, event | category | flops | bytes accessed | tf_op | source)
XLA Modules:
  0.0 116.9 jit_solution(15895574323645232349)
XLA Ops:
  0.7 15.6 %project_gather.1 = bf16[16,64,512]{2,1,0:T(8,128)(2,1)} custom-call(bf16[64,512]{1,0:T(8,128)(2,1)} %x_ref.1, bf16[512,512]{1,0:T(8,128)(2,1)} %w_ref.1), custom_call_target="tpu_custom_call" | custom-call | tf_op jit(solution)/shard_map/project_gather/pallas_call | solution.py:97
  16.3 15.0 %pair_messages.1.m_ref = f32[2048,512]{1,0:T(8,128)} custom-call(s32[1,1,12]{2,1,0:T(1,128)} %cells_ref.1, s32[1,1]{1,0:T(1,128)S(6)} %copy.13.count_ref, s32[256]{0:T(256)} %atoms_ref.3, f32[3,32768]{1,0:T(4,128)} %pos_ref.1, f32[16,512]{1,0:T(8,128)} %filter_ref.1, bf16[1024,512]{1,0:T(8,128)(2,1)} %bitcast.5), custom_call_target="tpu_custom_call" | custom-call | tf_op jit(solution)/shard_map/pair_messages/pallas_call | solution.py:199
  31.3 82.6 %sum_update_gather.1 = bf16[16,2,64,512]{3,2,1,0:T(8,128)(2,1)} custom-call(f32[2048,512]{1,0:T(8,128)} %pair_messages.1.m_ref, s32[256]{0:T(256)} %atoms_ref.3, bf16[512,512]{1,0:T(8,128)(2,1)} %hw_ref.1, f32[1,512]{1,0:T(1,128)} %bitcast.6, bf16[512,512]{1,0:T(8,128)(2,1)} %ow_ref.1, f32[1,512]{1,0:T(1,128)} %bitcast.7), custom_call_target="tpu_custom_call" | custom-call | tf_op jit(solution)/shard_map/sum_update_gather/pallas_call | solution.py:450
  113.9 3.0 %copy.14 = bf16[2048,512]{1,0:T(8,128)(2,1)} copy(bf16[2048,512]{1,0:T(8,128)(2,1)} %bitcast.4) | data formatting | bytes 4194304

commit v2 on v0

v2 whole, which is shorter than its diff:
```python
import functools
import math

import jax
import jax.numpy as jnp
from jax import lax
from jax.experimental import pallas as pl
from jax.experimental.pallas import tpu as pltpu
from jax.sharding import PartitionSpec as P

CL = 128
F = 512
NRBF = 16
CUTOFF = 5.0
MESH = pl.DeviceIdType.MESH
VMEM_LIMIT = 56 * 1024 * 1024


HALF = CL // 2
HF = F // 2


def vmem():
    return pl.BlockSpec(memory_space=pltpu.VMEM)


def smem():
    return pl.BlockSpec(memory_space=pltpu.SMEM)


def hbm():
    return pl.BlockSpec(memory_space=pl.ANY)


def envelope_of(squared):
    x = squared * (math.pi / (2.0 * CUTOFF)) ** 2
    coefficients = [(-1.0) ** n / math.factorial(2 * n) for n in range(8)]
    value = jnp.full_like(x, coefficients[-1])
    for c in coefficients[-2::-1]:
        value = value * x + c
    return value * value


def remote(src, dst, send, recv, device):
    return pltpu.make_async_remote_copy(
        src_ref=src,
        dst_ref=dst,
        send_sem=send,
        recv_sem=recv,
        device_id=device,
        device_id_type=MESH,
    )


def kernel(
    n_row,
    nz,
    clusters,
    slots,
    x_ref,
    pw_ref,
    cells_ref,
    count_ref,
    atoms_ref,
    pos_ref,
    filter_ref,
    hw_hbm,
    hb_ref,
    ow_hbm,
    ob_ref,
    out_ref,
    source,
    tpos,
    spos,
    tcols,
    srows,
    hw_ref,
    ow_ref,
    weights,
    scaled,
    jobs,
    xout,
    xin,
    tip_out,
    tip_in,
    far_in,
    near_in,
    zout,
    message,
    out_v,
    load_sem,
    row_send,
    row_recv,
    row_fwd,
    x_send,
    x_recv,
    tip_send,
    tip_recv,
    far_send,
    far_recv,
    near_send,
    near_recv,
    gx_send,
    gx_recv,
    gfar_send,
    gfar_recv,
    gnear_send,
    gnear_recv,
    out_sem,
):
    row = lax.axis_index("row")
    col = lax.axis_index("col")
    core = lax.rem(row, 2)
    chip = lax.div(row, 2)
    chips = n_row // 2
    h = lax.div(col, nz)
    z = lax.rem(col, nz)
    top = nz // 2
    ways = (0, 1)
    per_row = nz

    def in_row(index):
        return {"row": index}

    def in_col(index):
        return {"col": index}

    sibling = in_row(row + 1 - 2 * core)
    peers = [in_row(lax.rem(chip + j, chips) * 2 + core) for j in range(1, chips)]
    one = [
        in_col(h * nz + lax.rem(z + 1, nz)),
        in_col(h * nz + lax.rem(z + nz - 1, nz)),
    ]
    two = [
        in_col(h * nz + lax.rem(z + 2, nz)),
        in_col(h * nz + lax.rem(z + nz - 2, nz)),
    ]
    partner = in_col((1 - h) * nz + z)

    barrier = pltpu.get_barrier_semaphore()
    everyone = peers + [sibling] + one + two + [partner]
    for other in everyone:
        pl.semaphore_signal(barrier, inc=1, device_id=other, device_id_type=MESH)

    loads = [
        pltpu.make_async_copy(
            pos_ref.at[:, pl.ds(pl.multiple_of(row * per_row * CL, CL), per_row * CL)],
            tpos.at[pl.ds(0, 3)],
            load_sem.at[0],
        ),
        pltpu.make_async_copy(
            pos_ref.at[:, pl.ds(pl.multiple_of(col * clusters * CL, CL), clusters * CL)],
            spos.at[pl.ds(0, 3)],
            load_sem.at[1],
        ),
        pltpu.make_async_copy(hw_hbm, hw_ref, load_sem.at[2]),
        pltpu.make_async_copy(ow_hbm, ow_ref, load_sem.at[3]),
    ]
    tpos[...] = jnp.zeros_like(tpos)
    spos[...] = jnp.zeros_like(spos)
    for load in loads:
        load.start()

    source[chip, core] = jnp.dot(
        x_ref[...], pw_ref[...], preferred_element_type=jnp.float32
    ).astype(jnp.bfloat16)
    pl.semaphore_wait(barrier, len(everyone))

    def row_copy(c, k, send, device):
        ref = source.at[c, k]
        return remote(ref, ref, send, row_recv.at[c, k], device)

    def back(j):
        return lax.rem(chip + chips - j, chips)

    for j in range(1, chips):
        row_copy(chip, core, row_send.at[j], peers[j - 1]).start()
    row_copy(chip, core, row_fwd.at[0], sibling).start()

    targets = [lax.div(cells_ref[0, 0, slot], clusters) for slot in range(slots)]

    def last_of(t):
        found = slots
        for slot in range(slots):
            found = jnp.where(targets[slot] == t, slot, found)
        return found

    for q in range(2):
        jobs[q, slots] = jnp.zeros((CL, HF), jnp.float32)

    loads[0].wait()
    loads[1].wait()
    for t in range(per_row):
        tcols[t] = jnp.transpose(tpos[:, t * CL : (t + 1) * CL])
    for t in range(clusters):
        srows[t] = spos[:, t * CL : (t + 1) * CL]
    spread = math.sqrt(math.log2(math.e))

    def basis(slot, carry):
        cell = cells_ref[0, 0, slot]
        target = lax.div(cell, clusters)
        near_source = cell - target * clusters
        across = tcols[target]
        along = srows[near_source]
        squared = jnp.zeros((CL, CL), jnp.float32)
        for component in range(3):
            difference = across[:, component : component + 1] - along[component : component + 1, :]
            squared = squared + difference * difference
        distance = jnp.sqrt(squared)
        target_ids = (row * per_row + target) * CL + lax.broadcasted_iota(jnp.int32, (CL, CL), 0)
        local_ids = lax.broadcasted_iota(jnp.int32, (CL, CL), 1)
        source_cluster = col * clusters + near_source
        real = jnp.where(slot < count_ref[0, 0], atoms_ref[source_cluster], 0)
        allowed = (
            (target_ids != source_cluster * CL + local_ids)
            & (local_ids < real)
            & (distance < CUTOFF)
        )
        envelope = jnp.where(allowed, envelope_of(squared), 0.0)
        reach = distance * ((NRBF - 1) / CUTOFF * spread)
        for k in range(NRBF):
            offset = reach - k * spread
            weights[slot, :, k * CL : (k + 1) * CL] = (
                jnp.exp2(-(offset * offset)) * envelope
            ).astype(jnp.bfloat16)
        return carry

    early = slots * 2 // 3
    lax.fori_loop(0, early, basis, 0)
    for j in range(1, chips):
        row_copy(back(j), core, row_fwd.at[j], sibling).wait_recv()
        row_copy(back(j), core, row_fwd.at[j], sibling).start()
    lax.fori_loop(early, slots, basis, 0)
    for j in range(chips):
        row_copy(back(j), 1 - core, row_fwd.at[j], sibling).wait_recv()

    def ahead(way, d):
        return lax.rem(z + d, nz) if way == 0 else lax.rem(z + nz - d, nz)

    def behind(way, d):
        return ahead(1 - way, d)

    order = [(0, top)]
    for d in range(top - 1, 0, -2):
        pair = (d, d + 1) if d + 1 < top else (d,)
        order += [(way, e) for e in pair for way in ways]
    order += [(0, 0)]
    last = {(way, d): last_of(ahead(way, d)) for way, d in order}

    def mine(place, which, q):
        return jobs[q, last[place], pl.ds(pl.multiple_of(which * HALF, HALF), HALF), :]

    def x_copy(t, q):
        return remote(xout.at[t, q], xin.at[t, q], x_send.at[t, q], x_recv.at[t, q], partner)

    for q in range(2):
        columns = slice(q * HF, (q + 1) * HF)

        def scale(s, carry):
            rows = source[s, :, :, columns].reshape(CL, HF).astype(jnp.float32)
            for k in range(NRBF):
                scaled[s, k * CL : (k + 1) * CL, :] = (filter_ref[k : k + 1, columns] * rows).astype(
                    jnp.bfloat16
                )
            return carry

        lax.fori_loop(0, clusters, scale, 0)

        def job(slot, carry):
            cell = cells_ref[0, 0, slot]
            target = lax.div(cell, clusters)
            before = slots
            for other in range(slots - 1):
                before = jnp.where((targets[other] == target) & (other < slot), other, before)
            jobs[q, slot] = jobs[q, before] + jnp.dot(
                weights[slot],
                scaled[cell - target * clusters],
                preferred_element_type=jnp.float32,
            )
            return carry

        lax.fori_loop(0, slots, job, 0)
        for way, d in order:
            t = ahead(way, d)
            xout[t, q] = mine((way, d), 1 - h, q).astype(jnp.bfloat16)
            x_copy(t, q).start()

    def tip(q):
        return remote(tip_out.at[q], tip_in.at[q], tip_send.at[q], tip_recv.at[q], two[q])

    def near(way, d, q):
        i = (top - 1 - d) // 2
        return remote(
            zout.at[way, d - 1, q],
            near_in.at[way, i, q],
            near_send.at[way, i, q],
            near_recv.at[way, i, q],
            one[way],
        )

    def far(way, d, q):
        i = (top - 2 - d) // 2
        return remote(
            zout.at[way, d - 1, q],
            far_in.at[way, i, q],
            far_send.at[way, i, q],
            far_recv.at[way, i, q],
            two[way],
        )

    def come(way, d, q):
        near(way, d + 1, q).wait_recv()
        total = near_in[way, (top - 2 - d) // 2, q].astype(jnp.float32)
        if d + 2 == top:
            if way == q:
                tip(q).wait_recv()
                total = total + tip_in[q].astype(jnp.float32)
            return total
        far(way, d + 2, q).wait_recv()
        return total + far_in[way, (top - 4 - d) // 2, q].astype(jnp.float32)

    for q in range(2):
        for way, d in order:
            t = ahead(way, d)
            x_copy(t, q).wait_recv()
            total = mine((way, d), h, q) + xin[t, q].astype(jnp.float32)
            if d == top:
                tip_out[q] = total.astype(jnp.bfloat16)
                tip(q).start()
            elif d % 2:
                zout[way, d - 1, q] = total.astype(jnp.bfloat16)
                near(way, d, q).start()
            elif d:
                zout[way, d - 1, q] = (total + come(way, d, q)).astype(jnp.bfloat16)
                far(way, d, q).start()
            else:
                message[:, q * HF : (q + 1) * HF] = (total + come(0, 0, q) + come(1, 0, q)).astype(
                    jnp.bfloat16
                )

    loads[2].wait()
    loads[3].wait()
    hidden = jnp.dot(message[...], hw_ref[...], preferred_element_type=jnp.float32) + hb_ref[...]
    hidden = jnp.maximum(hidden, 0.0) + jnp.log1p(jnp.exp(-jnp.abs(hidden))) - math.log(2.0)
    result = (
        jnp.dot(hidden.astype(jnp.bfloat16), ow_ref[...], preferred_element_type=jnp.float32)
        + ob_ref[...]
    )
    atom = h * HALF + lax.broadcasted_iota(jnp.int32, (HALF, F), 0)
    valid = atoms_ref[row * per_row + z]
    out_v[z, h] = jnp.where(atom < valid, result, 0.0).astype(jnp.bfloat16)

    def g_near(way, e):
        ref = out_v.at[behind(way, e), h]
        i = e // 2
        return remote(ref, ref, gnear_send.at[way, i], gnear_recv.at[way, i], one[way])

    def g_far(way, e):
        i = e // 2
        if e + 2 == top:
            ref = out_v.at[behind(way, e), h, pl.ds(way * (HALF // 2), HALF // 2)]
        else:
            ref = out_v.at[behind(way, e), h]
        return remote(ref, ref, gfar_send.at[way, i], gfar_recv.at[way, i], two[way])

    def g_near_in(way, e):
        ref = out_v.at[behind(way, e + 1), h]
        i = e // 2
        remote(ref, ref, gnear_send.at[way, i], gnear_recv.at[way, i], one[way]).wait_recv()

    def g_far_in(way, e):
        i = e // 2
        if e + 2 == top:
            ref = out_v.at[behind(way, e + 2), h, pl.ds(way * (HALF // 2), HALF // 2)]
        else:
            ref = out_v.at[behind(way, e + 2), h]
        remote(ref, ref, gfar_send.at[way, i], gfar_recv.at[way, i], two[way]).wait_recv()

    def cross(t, which):
        ref = out_v.at[t, which]
        return remote(ref, ref, gx_send.at[t], gx_recv.at[t], partner)

    def store(t, which):
        return pltpu.make_async_copy(out_v.at[t, which], out_ref.at[t, which], out_sem.at[t, which])

    def keep(t):
        cross(t, h).start()
        store(t, h).start()

    for way in ways:
        g_far(way, 0).start()
    for way in ways:
        g_near(way, 0).start()
    keep(z)
    for e in range(2, top + 1, 2):
        for way in ways:
            g_far_in(way, e - 2)
            if e < top:
                g_far(way, e).start()
                g_near(way, e).start()
                keep(behind(way, e))
        if e == top:
            keep(behind(0, top))
        for way in ways:
            g_near_in(way, e - 2)
            keep(behind(way, e - 1))

    arrive = [z]
    for e in range(2, top, 2):
        arrive += [behind(way, e) for way in ways] + [behind(way, e - 1) for way in ways]
    arrive += [behind(0, top)] + [behind(way, top - 1) for way in ways]
    for t in arrive:
        cross(t, 1 - h).wait_recv()
        store(t, 1 - h).start()

    for j in range(1, chips):
        row_copy(chip, core, row_send.at[j], peers[j - 1]).wait_send()
    for j in range(chips):
        row_copy(back(j), core, row_fwd.at[j], sibling).wait_send()
    for w in ways:
        tip(w).wait_send()
        for q in range(2):
            for d in range(1, top):
                (near if d % 2 else far)(w, d, q).wait_send()
        for e in range(0, top, 2):
            g_near(w, e).wait_send()
            g_far(w, e).wait_send()

    def ended(t, carry):
        for which in range(2):
            x_copy(t, which).wait_send()
            store(t, which).wait()
        cross(t, h).wait_send()
        return carry

    lax.fori_loop(0, nz, ended, 0)


def local(
    n_row,
    n_col,
    features,
    positions,
    cluster_atoms,
    pair_cells,
    pair_count,
    project_weight,
    basis_filter,
    hidden_weight,
    hidden_bias,
    output_weight,
    output_bias,
):
    rows = features.shape[0]
    slots = pair_cells.shape[2]
    clusters = n_row * rows // CL
    nz = positions.shape[1] // CL // n_row
    top = nz // 2
    steps = top // 2
    bf16 = jnp.bfloat16
    dma = pltpu.SemaphoreType.DMA
    update = pl.pallas_call(
        functools.partial(kernel, n_row, nz, clusters, slots),
        out_shape=jax.ShapeDtypeStruct((nz, 2, HALF, F), bf16),
        in_specs=[
            vmem(),
            vmem(),
            smem(),
            smem(),
            smem(),
            hbm(),
            vmem(),
            hbm(),
            vmem(),
            hbm(),
            vmem(),
        ],
        out_specs=hbm(),
        scratch_shapes=[
            pltpu.VMEM((n_row // 2, 2, rows, F), bf16),
            pltpu.VMEM((8, nz * CL), jnp.float32),
            pltpu.VMEM((8, clusters * CL), jnp.float32),
            pltpu.VMEM((nz, CL, 8), jnp.float32),
            pltpu.VMEM((clusters, 8, CL), jnp.float32),
            pltpu.VMEM((F, F), bf16),
            pltpu.VMEM((F, F), bf16),
            pltpu.VMEM((slots, CL, NRBF * CL), bf16),
            pltpu.VMEM((clusters, NRBF * CL, HF), bf16),
            pltpu.VMEM((2, slots + 1, CL, HF), jnp.float32),
            pltpu.VMEM((nz, 2, HALF, HF), bf16),
            pltpu.VMEM((nz, 2, HALF, HF), bf16),
            pltpu.VMEM((2, HALF, HF), bf16),
            pltpu.VMEM((2, HALF, HF), bf16),
            pltpu.VMEM((2, steps - 1, 2, HALF, HF), bf16),
            pltpu.VMEM((2, steps, 2, HALF, HF), bf16),
            pltpu.VMEM((2, top - 1, 2, HALF, HF), bf16),
            pltpu.VMEM((HALF, F), bf16),
            pltpu.VMEM((nz, 2, HALF, F), bf16),
            dma((4,)),
            dma((n_row // 2,)),
            dma((n_row // 2, 2)),
            dma((n_row // 2,)),
            dma((nz, 2)),
            dma((nz, 2)),
            dma((2,)),
            dma((2,)),
            dma((2, steps - 1, 2)),
            dma((2, steps - 1, 2)),
            dma((2, steps, 2)),
            dma((2, steps, 2)),
            dma((nz,)),
            dma((nz,)),
            dma((2, steps)),
            dma((2, steps)),
            dma((2, steps)),
            dma((2, steps)),
            dma((nz, 2)),
        ],
        compiler_params=pltpu.CompilerParams(
            collective_id=0, has_side_effects=True, vmem_limit_bytes=VMEM_LIMIT
        ),
        name="interaction",
    )(
        features,
        project_weight,
        pair_cells,
        pair_count,
        cluster_atoms,
        positions,
        basis_filter,
        hidden_weight,
        hidden_bias.reshape(1, F),
        output_weight,
        output_bias.reshape(1, F),
    )
    return update.reshape(-1, F)


def solution(mesh):
    in_specs = (
        P(("col", "row"), None),
        P(),
        P(),
        P("row", "col", None),
        P("row", "col"),
        P(),
        P(),
        P(),
        P(),
        P(),
        P(),
    )
    out_specs = P("row", None)
    body = functools.partial(local, mesh.shape["row"], mesh.shape["col"])
    return jax.shard_map(body, mesh=mesh, in_specs=in_specs, out_specs=out_specs, check_vma=False)
```

time: 360 us -> 99.1 us (0.28)
  the two profiles are of different devices: /device:TPU:16 before, /device:TPU:64 now
where the time goes in v2:
time: 99.1 us; the launch traced here: 98.9 us
  Pallas kernels  95.2 us (96%)
  local copies, waits for them, and re-layouts  3.05 us (3%)
    pallas_call x1, Pallas kernels, local(): pl.pallas_call(functools.partial(kernel, n_row, nz, clusters, slots), out...  95.2 us
    unnamed x1, local copies, waits for them, and re-layouts  3.05 us

profile of v2, /device:TPU:64, one launch (start us, length us, event | category | flops | bytes accessed | tf_op | source)
XLA Modules:
  0.0 98.9 jit_solution(562870892188440460)
XLA Ops:
  0.7 95.2 %interaction.1 = bf16[16,2,64,512]{3,2,1,0:T(8,128)(2,1)} custom-call(bf16[64,512]{1,0:T(8,128)(2,1)} %x_ref.1, bf16[512,512]{1,0:T(8,128)(2,1)} %pw_ref.1, s32[1,1,12]{2,1,0:T(1,128)} %cells_ref.1, s32[1,1]{1,0:T(1,128)S(6)} %copy.13.count_ref, s32[256]{0:T(256)} %atoms_ref.1, f32[3,32768]{1,0:T(4,128)} %pos_ref.1, f32[16,512]{1,0:T(8,128)} %filter_ref.1, ...), custom_call_target="tpu_custom_call" | custom-call | tf_op jit(solution)/shard_map/interaction/pallas_call | solution.py:462
  95.9 3.0 %copy.14 = bf16[2048,512]{1,0:T(8,128)(2,1)} copy(bf16[2048,512]{1,0:T(8,128)(2,1)} %bitcast.3) | data formatting | bytes 4194304

commit v3 on v2

--- a/solution.py
+++ b/solution.py
@@ -225,14 +225,33 @@
             ).astype(jnp.bfloat16)
         return carry
 
+    def scale(c, k):
+        rows = source[c, k].astype(jnp.float32)
+        for n in range(NRBF):
+            for q in range(2):
+                columns = slice(q * HF, (q + 1) * HF)
+                scaled[q, c, n, k] = (filter_ref[n : n + 1, columns] * rows[:, columns]).astype(
+                    jnp.bfloat16
+                )
+
     early = slots * 2 // 3
     lax.fori_loop(0, early, basis, 0)
     for j in range(1, chips):
         row_copy(back(j), core, row_fwd.at[j], sibling).wait_recv()
         row_copy(back(j), core, row_fwd.at[j], sibling).start()
+
+    def scale_own(j, carry):
+        scale(back(j), core)
+        return carry
+
+    def scale_other(j, carry):
+        row_copy(back(j), 1 - core, row_fwd.at[0], sibling).wait_recv()
+        scale(back(j), 1 - core)
+        return carry
+
+    lax.fori_loop(0, chips, scale_own, 0)
     lax.fori_loop(early, slots, basis, 0)
-    for j in range(chips):
-        row_copy(back(j), 1 - core, row_fwd.at[j], sibling).wait_recv()
+    lax.fori_loop(0, chips, scale_other, 0)
 
     def ahead(way, d):
         return lax.rem(z + d, nz) if way == 0 else lax.rem(z + nz - d, nz)
@@ -240,11 +259,22 @@
     def behind(way, d):
         return ahead(1 - way, d)
 
-    order = [(0, top)]
-    for d in range(top - 1, 0, -2):
-        pair = (d, d + 1) if d + 1 < top else (d,)
-        order += [(way, e) for e in pair for way in ways]
-    order += [(0, 0)]
+    def both(q, *distances):
+        return [(q, way, d) for d in distances for way in (ways if 0 < d < top else (0,))]
+
+    odd = list(range(top - 1, 1, -2))
+    even = list(range(top - 4, 1, -2))
+    opening = (top, *odd, top - 2)
+    crossing = [both(0, *opening), both(1, *opening)]
+    work = both(0, top, *odd) + both(1, top, top - 1) + both(0, top - 2)
+    work += both(1, *odd[1:], top - 2)
+    for d in even:
+        raw = (1,) if d == even[0] else ()
+        crossing[1] += both(0, d, *raw) + both(1, d, *raw)
+        work += both(0, d, *raw) + both(1, *raw, d)
+    crossing[1] += both(0, 0) + both(1, 0)
+    work += both(0, 0) + both(1, 0)
+    order = [(way, d) for q, way, d in work if q == 0]
     last = {(way, d): last_of(ahead(way, d)) for way, d in order}
 
     def mine(place, which, q):
@@ -254,18 +284,6 @@
         return remote(xout.at[t, q], xin.at[t, q], x_send.at[t, q], x_recv.at[t, q], partner)
 
     for q in range(2):
-        columns = slice(q * HF, (q + 1) * HF)
-
-        def scale(s, carry):
-            rows = source[s, :, :, columns].reshape(CL, HF).astype(jnp.float32)
-            for k in range(NRBF):
-                scaled[s, k * CL : (k + 1) * CL, :] = (filter_ref[k : k + 1, columns] * rows).astype(
-                    jnp.bfloat16
-                )
-            return carry
-
-        lax.fori_loop(0, clusters, scale, 0)
-
         def job(slot, carry):
             cell = cells_ref[0, 0, slot]
             target = lax.div(cell, clusters)
@@ -274,16 +292,16 @@
                 before = jnp.where((targets[other] == target) & (other < slot), other, before)
             jobs[q, slot] = jobs[q, before] + jnp.dot(
                 weights[slot],
-                scaled[cell - target * clusters],
+                scaled[q, cell - target * clusters].reshape(NRBF * CL, HF),
                 preferred_element_type=jnp.float32,
             )
             return carry
 
         lax.fori_loop(0, slots, job, 0)
-        for way, d in order:
+        for p, way, d in crossing[q]:
             t = ahead(way, d)
-            xout[t, q] = mine((way, d), 1 - h, q).astype(jnp.bfloat16)
-            x_copy(t, q).start()
+            xout[t, p] = mine((way, d), 1 - h, p).astype(jnp.bfloat16)
+            x_copy(t, p).start()
 
     def tip(q):
         return remote(tip_out.at[q], tip_in.at[q], tip_send.at[q], tip_recv.at[q], two[q])
@@ -319,24 +337,23 @@
         far(way, d + 2, q).wait_recv()
         return total + far_in[way, (top - 4 - d) // 2, q].astype(jnp.float32)
 
-    for q in range(2):
-        for way, d in order:
-            t = ahead(way, d)
-            x_copy(t, q).wait_recv()
-            total = mine((way, d), h, q) + xin[t, q].astype(jnp.float32)
-            if d == top:
-                tip_out[q] = total.astype(jnp.bfloat16)
-                tip(q).start()
-            elif d % 2:
-                zout[way, d - 1, q] = total.astype(jnp.bfloat16)
-                near(way, d, q).start()
-            elif d:
-                zout[way, d - 1, q] = (total + come(way, d, q)).astype(jnp.bfloat16)
-                far(way, d, q).start()
-            else:
-                message[:, q * HF : (q + 1) * HF] = (total + come(0, 0, q) + come(1, 0, q)).astype(
-                    jnp.bfloat16
-                )
+    for q, way, d in work:
+        t = ahead(way, d)
+        x_copy(t, q).wait_recv()
+        total = mine((way, d), h, q) + xin[t, q].astype(jnp.float32)
+        if d == top:
+            tip_out[q] = total.astype(jnp.bfloat16)
+            tip(q).start()
+        elif d % 2:
+            zout[way, d - 1, q] = total.astype(jnp.bfloat16)
+            near(way, d, q).start()
+        elif d:
+            zout[way, d - 1, q] = (total + come(way, d, q)).astype(jnp.bfloat16)
+            far(way, d, q).start()
+        else:
+            message[:, q * HF : (q + 1) * HF] = (total + come(0, 0, q) + come(1, 0, q)).astype(
+                jnp.bfloat16
+            )
 
     loads[2].wait()
     loads[3].wait()
@@ -485,7 +502,7 @@
             pltpu.VMEM((F, F), bf16),
             pltpu.VMEM((F, F), bf16),
             pltpu.VMEM((slots, CL, NRBF * CL), bf16),
-            pltpu.VMEM((clusters, NRBF * CL, HF), bf16),
+            pltpu.VMEM((2, clusters, NRBF, 2, HALF, HF), bf16),
             pltpu.VMEM((2, slots + 1, CL, HF), jnp.float32),
             pltpu.VMEM((nz, 2, HALF, HF), bf16),
             pltpu.VMEM((nz, 2, HALF, HF), bf16),

time: 99.1 us -> 91.9 us (0.927)
  the two profiles are of different devices: /device:TPU:64 before, /device:TPU:32 now
where the time goes in v3:
time: 91.9 us; the launch traced here: 91.7 us
  Pallas kernels  88 us (96%)
  local copies, waits for them, and re-layouts  3.05 us (3%)
    pallas_call x1, Pallas kernels, local(): pl.pallas_call(functools.partial(kernel, n_row, nz, clusters, slots), out...  88 us
    unnamed x1, local copies, waits for them, and re-layouts  3.05 us

profile of v3, /device:TPU:32, one launch (start us, length us, event | category | flops | bytes accessed | tf_op | source)
XLA Modules:
  0.0 91.7 jit_solution(15984592182026869765)
XLA Ops:
  0.7 88.0 %interaction.1 = bf16[16,2,64,512]{3,2,1,0:T(8,128)(2,1)} custom-call(bf16[64,512]{1,0:T(8,128)(2,1)} %x_ref.1, bf16[512,512]{1,0:T(8,128)(2,1)} %pw_ref.1, s32[1,1,12]{2,1,0:T(1,128)} %cells_ref.1, s32[1,1]{1,0:T(1,128)S(6)} %copy.13.count_ref, s32[256]{0:T(256)} %atoms_ref.1, f32[3,32768]{1,0:T(4,128)} %pos_ref.1, f32[16,512]{1,0:T(8,128)} %filter_ref.1, ...), custom_call_target="tpu_custom_call" | custom-call | tf_op jit(solution)/shard_map/interaction/pallas_call | solution.py:479
  88.7 3.0 %copy.14 = bf16[2048,512]{1,0:T(8,128)(2,1)} copy(bf16[2048,512]{1,0:T(8,128)(2,1)} %bitcast.3) | data formatting | bytes 4194304
